TPU v7x, 32 devices: a whole 2x2x4 slice. The times are simulated.
32 devices in a mesh: ens: 2 (over y), lon: 8 (over z, x), lat: 2 (over core).
Axes of the slice: x: 2, y: 2, z: 4, core: 2. Of those that a mesh axis runs over, the one named last changes fastest.
Arguments:
- state_in: float32 [1024, 128, 256], P(('ens', 'lon'), 'lat'), parts along dimension 0, may hold values from -6 to 6
- diffusion: float32 [256], replicated, may hold values from 0.2 to 0.245
- conv_index: int32 [16, 2, 3072], P(('ens', 'lon'), 'lat'), parts along dimension 0, may hold values from 0 to 4095, as said below
- conv_count: int32 [2, 8, 2], P('ens', None, 'lat'), parts along dimension 0, may hold values from 8 to 3072, as said below
- w_first: bfloat16 [256, 1024], replicated, may hold values from -0.375 to 0.375
- w_hidden: bfloat16 [2, 1024, 1024], replicated, may hold values from -0.1875 to 0.1875
- w_last: bfloat16 [1024, 256], replicated, may hold values from -0.1875 to 0.1875
Outputs:
- state_out: float32 [1024, 128, 256], P(('ens', 'lon'), 'lat'), parts along dimension 0
There are 2 independent parts, one for each index of `ens`. A program takes and returns all parts, laid end to end along the dimension named above; an argument that names none is the same for every part. Nothing has to cross between parts.
Inputs may be any that keep to these rules, and one draw needn't show every extreme that they name: `conv_index`: each device's list holds 3072 distinct local column numbers a * 64 + b for row a and place b of its block; only the first conv_count entries are convecting. `conv_count`: entry [0, l, m] counts the convecting columns of the device at lon index l and lat index m. Each count is a whole multiple of the number of lon devices, and the counts of one latitude band average exactly 1344.
All inputs are finite; a program needn't handle non-finite values.
Results may differ from a plain program's by a relative error of at most 0.0003.
Values may be sent and summed in bfloat16 or wider, within the bound.
A program may use at most 128 MiB of HBM per device.

v0:
```python
import functools

import jax
import jax.numpy as jnp
from jax import lax
from jax.experimental import pallas as pl
from jax.experimental.pallas import tpu as pltpu
from jax.sharding import PartitionSpec as P

HALO = 4
BLOCK = 8
PAD = 8
ALIGN = 16
TILE = 256
ROWS = 512
LANES = 128


def silu(u):
    half = 0.5 * u
    return half + half * jnp.tanh(half)


def kernel(
    state, north, south, side, corner_n, corner_s, diffusion, keys, offs,
    w_first, w_hidden, w_last, out,
    a_buf, b_buf, packed, hid_a, hid_b, w1, wh, w3, rows_in, in_sem, w_sem, out_sem,
):
    lon, lat, feat = state.shape
    lanes = feat // 2
    me = lax.axis_index("lat")
    own = pl.multiple_of(PAD + BLOCK * me, BLOCK)
    beside = pl.multiple_of(jnp.where(me == 0, PAD + lat, PAD), BLOCK)
    top, low = HALO, HALO + lon

    copies = []
    for half in range(2):
        cut = pl.ds(half * lanes, lanes)
        for source, row, rows, place, width in (
            (side, top, lon, beside, BLOCK),
            (corner_n, 0, HALO, beside, BLOCK),
            (corner_s, low, HALO, beside, BLOCK),
            (state, top, lon, own, lat),
        ):
            copies.append(
                pltpu.make_async_copy(
                    source.at[:, :, cut],
                    a_buf.at[half, pl.ds(row, rows), pl.ds(place, width), :],
                    in_sem.at[len(copies)],
                )
            )
    for source, which in ((north, 0), (south, 1)):
        copies.append(pltpu.make_async_copy(source, rows_in.at[which], in_sem.at[len(copies)]))
    weights = [
        pltpu.make_async_copy(w_first, w1, w_sem.at[0]),
        pltpu.make_async_copy(w_hidden, wh, w_sem.at[1]),
        pltpu.make_async_copy(w_last, w3, w_sem.at[2]),
    ]
    for copy in copies:
        copy.start()
    for copy in weights:
        copy.start()
    wide = a_buf.shape[2] - 2 * PAD

    def clear(row, carry):
        for buf in (a_buf, b_buf):
            for half in range(2):
                buf[half, row, 0:PAD, :] = jnp.zeros((PAD, lanes), jnp.float32)
                buf[half, row, PAD + wide :, :] = jnp.zeros((PAD, lanes), jnp.float32)
        return carry

    lax.fori_loop(0, a_buf.shape[1], clear, 0)
    for copy in copies:
        copy.wait()
    for which, row in ((0, 0), (1, low)):
        for half in range(2):
            cells = rows_in[which, :, :, half * lanes : (half + 1) * lanes].astype(jnp.float32)
            a_buf[half, row : row + HALO, pl.ds(own, lat), :] = cells

    def sweep(src, dst, first, last):
        def row_step(row, carry):
            for half in range(2):
                amount = diffusion[0:1, half * lanes : (half + 1) * lanes]
                keep = 1.0 - 4.0 * amount
                here = src[half, row, PAD : PAD + wide, :]
                around = (
                    src[half, row - 1, PAD : PAD + wide, :]
                    + src[half, row + 1, PAD : PAD + wide, :]
                ) + (
                    src[half, row, PAD - 1 : PAD + wide - 1, :]
                    + src[half, row, PAD + 1 : PAD + wide + 1, :]
                )
                dst[half, row, PAD : PAD + wide, :] = keep * here + amount * around
            return carry

        lax.fori_loop(first, last, row_step, 0)

    sweep(a_buf, b_buf, 1, low + HALO - 1)
    sweep(b_buf, a_buf, 2, low + HALO - 2)

    per_tile = TILE // lat
    pieces = [
        [(HALO - 1, 1, beside, BLOCK), (low, 1, beside, BLOCK)],
        [(top, lon // 2, beside, BLOCK)],
        [(top + lon // 2, lon // 2, beside, BLOCK)],
        [(HALO - 2, 2, own, lat), (low, 2, own, lat)],
    ]
    n_side = len(pieces)
    n_main = lon // per_tile

    def select(tile, width):
        spot = lax.broadcasted_iota(jnp.int32, (TILE, width), 0).astype(jnp.float32)
        return jnp.where(spot == keys[pl.ds(tile, 1), 0:width], 1.0, 0.0).astype(jnp.bfloat16)

    def gather(tile, slices):
        halves = [
            jnp.concatenate(
                [
                    a_buf[half, pl.ds(row, rows), pl.ds(place, width), :].reshape(rows * width, lanes)
                    for row, rows, place, width in slices
                ],
                axis=0,
            ).astype(jnp.bfloat16)
            for half in range(2)
        ]
        values = jnp.concatenate(halves, axis=1)
        picked = jnp.dot(select(tile, values.shape[0]), values, preferred_element_type=jnp.float32)
        start = pl.multiple_of(offs[tile], ALIGN)
        packed[pl.ds(start, TILE), :] = picked.astype(jnp.bfloat16)

    def scatter(tile, slices):
        start = pl.multiple_of(offs[tile], ALIGN)
        change = packed[pl.ds(start, TILE), :]
        count = sum(rows * width for _, rows, _, width in slices)
        spread = lax.dot_general(
            select(tile, count), change, (((0,), (0,)), ((), ())), preferred_element_type=jnp.float32
        )
        for half in range(2):
            done = 0
            for row, rows, place, width in slices:
                part = spread[done : done + rows * width, half * lanes : (half + 1) * lanes]
                done += rows * width
                where = (half, pl.ds(row, rows), pl.ds(place, width), slice(None))
                a_buf[where] = a_buf[where] + part.reshape(rows, width, lanes)

    for tile, slices in enumerate(pieces):
        gather(tile, slices)

    def main_gather(step, carry):
        gather(n_side + step, [(top + per_tile * step, per_tile, own, lat)])
        return carry

    lax.fori_loop(0, n_main, main_gather, 0, unroll=2)
    for copy in weights:
        copy.wait()

    hidden = w1.shape[1]

    def layer(x, weight, dst):
        for column in range(0, hidden, TILE):
            u = jnp.dot(x, weight[:, column : column + TILE], preferred_element_type=jnp.float32)
            dst[:, column : column + TILE] = silu(u).astype(jnp.bfloat16)

    def network(step, carry):
        rows = pl.ds(pl.multiple_of(step * ROWS, ROWS), ROWS)
        layer(packed[rows, :], w1, hid_a)
        now, other = hid_a, hid_b
        for middle in range(wh.shape[0]):
            layer(now[...], wh.at[middle], other)
            now, other = other, now
        packed[rows, :] = jnp.dot(now[...], w3[...], preferred_element_type=jnp.float32).astype(
            jnp.bfloat16
        )
        return carry

    total = offs[n_side + n_main]
    lax.fori_loop(0, (total + ROWS - 1) // ROWS, network, 0)

    for tile, slices in enumerate(pieces):
        scatter(tile, slices)

    def main_scatter(step, carry):
        scatter(n_side + step, [(top + per_tile * step, per_tile, own, lat)])
        return carry

    lax.fori_loop(0, n_main, main_scatter, 0, unroll=2)

    sweep(a_buf, b_buf, 3, low + HALO - 3)
    parts = 4
    outs = []
    for part in range(parts):
        begin = part * lon // parts
        size = (part + 1) * lon // parts - begin
        sweep(b_buf, a_buf, top + begin, top + begin + size)
        for half in range(2):
            copy = pltpu.make_async_copy(
                a_buf.at[half, pl.ds(top + begin, size), pl.ds(own, lat), :],
                out.at[pl.ds(begin, size), :, pl.ds(half * lanes, lanes)],
                out_sem.at[len(outs)],
            )
            copy.start()
            outs.append(copy)
    for copy in outs:
        copy.wait()


def exchange(
    n_lon, state, listed, counts,
    north, south, side, corner_n, corner_s, mask, other, above, below, above_x, below_x,
    edges, lines, edge_sem, send_sem, recv_sem,
):
    lon, lat, _ = state.shape
    place, me = lax.axis_index("lon"), lax.axis_index("lat")
    east, west, across = lax.rem(place + 1, n_lon), lax.rem(place + n_lon - 1, n_lon), 1 - me
    others = [(west, me), (east, me), (place, across), (west, across), (east, across)]

    def device(spot):
        return {"lon": spot[0], "lat": spot[1]}

    loads = [
        pltpu.make_async_copy(state.at[pl.ds(row, HALO)], edges.at[which], edge_sem.at[which])
        for which, row in ((0, 0), (1, lon - HALO))
    ]
    for load in loads:
        load.start()
    barrier = pltpu.get_barrier_semaphore()
    for spot in others:
        pl.semaphore_signal(
            barrier, inc=1, device_id=device(spot), device_id_type=pl.DeviceIdType.MESH
        )
    pl.semaphore_wait(barrier, len(others))

    sent = []

    def send(source, target, spot):
        copy = pltpu.make_async_remote_copy(
            src_ref=source,
            dst_ref=target,
            send_sem=send_sem.at[len(sent)],
            recv_sem=recv_sem.at[len(sent)],
            device_id=device(spot),
            device_id_type=pl.DeviceIdType.MESH,
        )
        copy.start()
        sent.append(copy)

    for which, target, spot in ((0, south, others[0]), (1, north, others[1])):
        loads[which].wait()
        lines[which] = edges[which].astype(jnp.bfloat16)
        send(lines.at[which], target, spot)
    cut = pl.ds(pl.multiple_of(jnp.where(me == 0, lat - BLOCK, 0), BLOCK), BLOCK)
    send(state.at[pl.ds(0, HALO), cut], corner_s, others[3])
    send(state.at[pl.ds(lon - HALO, HALO), cut], corner_n, others[4])
    send(state.at[:, cut], side, others[2])

    numbers = listed[...]
    length = numbers.shape[1]
    active = lax.broadcasted_iota(jnp.int32, (1, length), 1) < counts[place]
    rows = jnp.where(active, lax.shift_right_logical(numbers, jnp.int32(lat.bit_length() - 1)), -1)
    spots = numbers & (lat - 1)
    row_hot = jnp.where(lax.broadcasted_iota(jnp.int32, (lon, length), 0) == rows, 1.0, 0.0)
    spot_hot = jnp.where(lax.broadcasted_iota(jnp.int32, (LANES, length), 0) == spots, 1.0, 0.0)
    mask[...] = lax.dot_general(
        row_hot.astype(jnp.bfloat16), spot_hot.astype(jnp.bfloat16), (((1,), (1,)), ((), ())),
        preferred_element_type=jnp.float32,
    )
    first, last = mask.at[pl.ds(0, BLOCK)], mask.at[pl.ds(lon - BLOCK, BLOCK)]
    send(mask, other, others[2])
    send(first, below, others[0])
    send(last, above, others[1])
    send(first, below_x, others[3])
    send(last, above_x, others[4])
    for copy in sent:
        copy.wait()


def take_near(rows, lat, first_lat):
    reach = jnp.arange(BLOCK)
    near = jnp.where(first_lat, rows[:, :BLOCK], rows[:, lat - BLOCK : lat])
    return jnp.where(jnp.where(first_lat, reach < 2, reach >= BLOCK - 2)[None], near, 0.0)


def local(n_lon, state_in, diffusion, conv_index, conv_count, w_first, w_hidden, w_last):
    lon, lat, feat = state_in.shape
    lat_place = lax.axis_index("lat")
    first_lat = lat_place == 0

    listed = conv_index.reshape(1, -1)
    anywhere = pl.BlockSpec(memory_space=pl.ANY)
    vmem = pl.BlockSpec(memory_space=pltpu.VMEM)
    smem = pl.BlockSpec(memory_space=pltpu.SMEM)
    shape = jax.ShapeDtypeStruct
    lines = shape((HALO, lat, feat), jnp.bfloat16)
    block = shape((HALO, BLOCK, feat), jnp.float32)
    few = shape((BLOCK, LANES), jnp.float32)
    full = shape((lon, LANES), jnp.float32)
    north, south, side, corner_n, corner_s, mask, other, above, below, above_x, below_x = pl.pallas_call(
        functools.partial(exchange, n_lon),
        out_shape=(lines, lines, shape((lon, BLOCK, feat), jnp.float32), block, block)
        + (full, full, few, few, few, few),
        in_specs=[anywhere, vmem, smem],
        out_specs=(anywhere,) * 5 + (vmem,) * 6,
        scratch_shapes=[
            pltpu.VMEM((2, HALO, lat, feat), jnp.float32),
            pltpu.VMEM((2, HALO, lat, feat), jnp.bfloat16),
            pltpu.SemaphoreType.DMA((2,)),
            pltpu.SemaphoreType.DMA((10,)),
            pltpu.SemaphoreType.DMA((10,)),
        ],
        compiler_params=pltpu.CompilerParams(collective_id=0, has_side_effects=True),
    )(state_in, listed, conv_count[0, :, 0])
    mask = mask[:, :lat]
    other = other[:, :lat]
    above = jnp.concatenate([above[BLOCK - 2 :, :lat], take_near(above_x[BLOCK - 2 :], lat, first_lat)], axis=1)
    below = jnp.concatenate([below[:2, :lat], take_near(below_x[:2], lat, first_lat)], axis=1)
    near = take_near(other, lat, first_lat)
    corner = jnp.concatenate([above[1, lat:], below[0, lat:]])
    tiles = jnp.concatenate(
        [
            jnp.pad(corner, (0, TILE - corner.shape[0]))[None],
            near.reshape(-1, TILE),
            jnp.concatenate([above[:, :lat], below[:, :lat]]).reshape(-1, TILE),
            mask.reshape(-1, TILE),
        ]
    )
    spots = jnp.arange(TILE)
    ranks = jnp.dot(
        tiles.astype(jnp.bfloat16),
        (spots[:, None] < spots[None]).astype(jnp.bfloat16),
        preferred_element_type=jnp.float32,
    )
    keys = jnp.where(tiles > 0.5, ranks, -1.0)
    counts = tiles.sum(axis=1).astype(jnp.int32)
    counts = (counts + ALIGN - 1) // ALIGN * ALIGN
    n_tiles = tiles.shape[0]
    order = jnp.arange(n_tiles + 1)
    offs = jnp.where(order[:n_tiles][None] < order[:, None], counts[None], 0).sum(axis=1)

    room = -(-(n_tiles * TILE + TILE) // ROWS) * ROWS
    wide = lat + BLOCK + 2 * PAD
    buf = pltpu.VMEM((2, lon + 2 * HALO, wide, feat // 2), jnp.float32)
    hidden = w_first.shape[1]
    return pl.pallas_call(
        kernel,
        out_shape=jax.ShapeDtypeStruct(state_in.shape, jnp.float32),
        in_specs=[anywhere] * 6 + [vmem, vmem, smem] + [anywhere] * 3,
        out_specs=anywhere,
        scratch_shapes=[
            buf,
            buf,
            pltpu.VMEM((room, feat), jnp.bfloat16),
            pltpu.VMEM((ROWS, hidden), jnp.bfloat16),
            pltpu.VMEM((ROWS, hidden), jnp.bfloat16),
            pltpu.VMEM(w_first.shape, jnp.bfloat16),
            pltpu.VMEM(w_hidden.shape, jnp.bfloat16),
            pltpu.VMEM(w_last.shape, jnp.bfloat16),
            pltpu.VMEM((2,) + north.shape, jnp.bfloat16),
            pltpu.SemaphoreType.DMA((10,)),
            pltpu.SemaphoreType.DMA((3,)),
            pltpu.SemaphoreType.DMA((8,)),
        ],
        compiler_params=pltpu.CompilerParams(vmem_limit_bytes=50 * 1024 * 1024),
    )(
        state_in, north, south, side, corner_n, corner_s, diffusion[None], keys, offs,
        w_first, w_hidden, w_last,
    )


def solution(mesh):
    return jax.shard_map(
        functools.partial(local, mesh.shape["lon"]),
        mesh=mesh,
        in_specs=(
            P(("ens", "lon"), "lat", None),
            P(),
            P(("ens", "lon"), "lat", None),
            P("ens", None, "lat"),
            P(),
            P(),
            P(),
        ),
        out_specs=P(("ens", "lon"), "lat", None),
        check_vma=False,
    )
```

profile of v0, /device:TPU:5, one launch (start us, length us, event | category | flops | bytes accessed | tf_op | source)
XLA Modules:
  0.0 60.9 jit_solution(18420298186956813973)
XLA Ops:
  0.0 0.0 copy-start.1
  0.0 0.0 copy-start.7
  0.0 13.3 %shard_map.73 = (bf16[4,64,256]{2,1,0:T(8,128)(2,1)}, bf16[4,64,256]{2,1,0:T(8,128)(2,1)}, f32[64,8,256]{2,1,0:T(8,128)}, f32[4,8,256]{2,1,0:T(8,128)}, f32[4,8,...) custom-call(f32[64,64,256]{2,1,0:T(8,128)} %state.3, ...), custom_call_target="tpu_custom_call" | custom-call | tf_op jit(solution)/shard_map/pallas_call | solution.py:297
  13.4 0.7 %slice.53 = f32[2,64]{1,0:T(2,128)S(1)} slice(f32[8,128]{1,0:T(8,128)} %get-tuple-element.24), slice={[6:8], [0:64]} | slice | bytes 1024 | tf_op jit(solution)/shard_map/slice | solution.py:314
  14.1 0.7 %slice.54 = f32[2,64]{1,0:T(2,128)S(1)} slice(f32[8,128]{1,0:T(8,128)} %get-tuple-element.25), slice={[0:2], [0:64]} | slice | bytes 1024 | tf_op jit(solution)/shard_map/slice | solution.py:315
  14.8 0.1 reshape.42
  14.9 0.8 %select_select_fusion.2 = (f32[2,8]{1,0:T(2,128)S(1)}, f32[2,8]{1,0:T(2,128)S(1)}) fusion(f32[8,128]{1,0:T(8,128)} %get-tuple-element.21, pred[]{:T(512)S(6)} %eq.3, pred[8]{0:T(512)(128)(4,1)S(1)} %compare_select_fusion, f32[8,128]{1,0:T(8,128)} %get-tuple-element.22), kind=kLoop, calls=%fused_computation.16 | loop fusion | flops 64 | bytes 393 | tf_op jit(solution)/shard_map/jit(_where)/select_n | solution.py:280
  15.7 0.9 %select_select_fusion = f32[64,8]{1,0:T(8,128)S(1)} fusion(f32[64,128]{1,0:T(8,128)} %get-tuple-element.23, pred[]{:T(512)S(6)} %eq.3, pred[8]{0:T(512)(128)(4,1)S(1)} %compare_select_fusion), kind=kLoop, calls=%fused_computation.2 | loop fusion | flops 1024 | bytes 6153 | tf_op jit(solution)/shard_map/jit(_where)/select_n | solution.py:280
  16.6 0.1 reshape.41
  16.7 0.1 select_maximum_fusion
  16.8 0.8 %reshape.43 = f32[16,256]{1,0:T(8,128)S(1)} reshape(f32[64,64]{1,0:T(8,128)} %bitcast.11) | data formatting | bytes 32768 | tf_op jit(solution)/shard_map/reshape | solution.py:323
  17.6 0.1 fusion.1
  17.7 0.1 select_reduce_fusion.offs
  17.8 0.2 convolution_select_fusion.keys
  18.0 0.0 copy-done.1
  18.0 0.0 copy-done
  18.0 0.0 copy-done.7
  18.0 0.0 copy-start.2
  18.0 1.0 %copy-done.2 = f32[64,8,256]{2,1,0:T(8,128)S(1)} copy-done((f32[64,8,256]{2,1,0:T(8,128)S(1)}, f32[64,8,256]{2,1,0:T(8,128)}, u32[]{:S(2)}) %copy-start.2) | copy-done | bytes 524312
  19.1 0.9 %copy-done.3 = bf16[4,64,256]{2,1,0:T(8,128)(2,1)S(1)} copy-done((bf16[4,64,256]{2,1,0:T(8,128)(2,1)S(1)}, bf16[4,64,256]{2,1,0:T(8,128)(2,1)}, u32[]{:S(2)}) %copy-start.3) | copy-done | bytes 131096
  20.0 0.9 %copy-done.4 = bf16[4,64,256]{2,1,0:T(8,128)(2,1)S(1)} copy-done((bf16[4,64,256]{2,1,0:T(8,128)(2,1)S(1)}, bf16[4,64,256]{2,1,0:T(8,128)(2,1)}, u32[]{:S(2)}) %copy-start.4) | copy-done | bytes 131096
  20.9 0.8 %copy-done.5 = f32[4,8,256]{2,1,0:T(8,128)S(1)} copy-done((f32[4,8,256]{2,1,0:T(8,128)S(1)}, f32[4,8,256]{2,1,0:T(8,128)}, u32[]{:S(2)}) %copy-start.5) | copy-done | bytes 32792
  21.6 0.8 %copy-done.6 = f32[4,8,256]{2,1,0:T(8,128)S(1)} copy-done((f32[4,8,256]{2,1,0:T(8,128)S(1)}, f32[4,8,256]{2,1,0:T(8,128)}, u32[]{:S(2)}) %copy-start.6) | copy-done | bytes 32792
  22.4 38.5 %shard_map.74 = f32[64,64,256]{2,1,0:T(8,128)} custom-call(f32[64,64,256]{2,1,0:T(8,128)} %state.3, bf16[4,64,256]{2,1,0:T(8,128)(2,1)S(1)} %copy-done.3, bf16[4,64,256]{2,1,0:T(8,128)(2,1)S(1)} %copy-done.4, f32[64,8,256]{2,1,0:T(8,128)S(1)} %copy-done.2, f32[4,8,256]{2,1,0:T(8,128)S(1)} %copy-done.5, f32[4,8,256]{2,1,0:T(8,128)S(1)} %copy-done.6, ...), custom_call_target="tpu_custom_call" | custom-call | tf_op jit(solution)/shard_map/pallas_call | solution.py:343
  (10 shorter events, 0.0 us)
Async XLA Ops:
  0.0 18.0 %copy-start.1 = (bf16[1024,256]{1,0:T(8,128)(2,1)S(1)}, bf16[1024,256]{1,0:T(8,128)(2,1)}, u32[]{:S(2)}) copy-start(bf16[1024,256]{1,0:T(8,128)(2,1)} %w_last.1) | copy-start | bytes 1572868
  0.0 18.0 %copy-start = (bf16[256,1024]{1,0:T(8,128)(2,1)S(1)}, bf16[256,1024]{1,0:T(8,128)(2,1)}, u32[]{:S(2)}) copy-start(bf16[256,1024]{1,0:T(8,128)(2,1)} %w_first.1) | copy-start | bytes 1572868
  0.0 18.0 %copy-start.7 = (f32[256]{0:T(256)S(1)}, f32[256]{0:T(256)}, u32[]{:S(2)}) copy-start(f32[256]{0:T(256)} %param.8) | copy-start | bytes 3076
  18.0 1.0 %copy-start.2 = (f32[64,8,256]{2,1,0:T(8,128)S(1)}, f32[64,8,256]{2,1,0:T(8,128)}, u32[]{:S(2)}) copy-start(f32[64,8,256]{2,1,0:T(8,128)} %get-tuple-element.18.side) | copy-start | bytes 1572868
  19.1 0.9 %copy-start.3 = (bf16[4,64,256]{2,1,0:T(8,128)(2,1)S(1)}, bf16[4,64,256]{2,1,0:T(8,128)(2,1)}, u32[]{:S(2)}) copy-start(bf16[4,64,256]{2,1,0:T(8,128)(2,1)} %get-tuple-element.16.north) | copy-start | bytes 393220
  20.0 0.9 %copy-start.4 = (bf16[4,64,256]{2,1,0:T(8,128)(2,1)S(1)}, bf16[4,64,256]{2,1,0:T(8,128)(2,1)}, u32[]{:S(2)}) copy-start(bf16[4,64,256]{2,1,0:T(8,128)(2,1)} %get-tuple-element.17.south) | copy-start | bytes 393220
  20.9 0.8 %copy-start.5 = (f32[4,8,256]{2,1,0:T(8,128)S(1)}, f32[4,8,256]{2,1,0:T(8,128)}, u32[]{:S(2)}) copy-start(f32[4,8,256]{2,1,0:T(8,128)} %get-tuple-element.19.corner_n) | copy-start | bytes 98308
  21.6 0.8 %copy-start.6 = (f32[4,8,256]{2,1,0:T(8,128)S(1)}, f32[4,8,256]{2,1,0:T(8,128)}, u32[]{:S(2)}) copy-start(f32[4,8,256]{2,1,0:T(8,128)} %get-tuple-element.20.corner_s) | copy-start | bytes 98308
where the time goes:
time: 61.5 us; the launch traced here: 60.9 us
  Pallas kernels  51.9 us (84%)
  local copies, waits for them, and re-layouts  6.75 us (11%)
  other arithmetic  2.06 us (3%)
    pallas_call x1, Pallas kernels, local(): pl.pallas_call(kernel, out_shape=jax.ShapeDtypeStruct(state_in.shape, jnp...  38.5 us
    pallas_call x1, Pallas kernels, local(): pl.pallas_call(functools.partial(exchange, n_lon), out_shape=(lines, line...  13.3 us
    unnamed x16, local copies, waits for them, and re-layouts  4.37 us
    select_n x2, other arithmetic, take_near(): jnp.where(jnp.where(first_lat, reach < 2, reach >= BLOCK - 2)[None], near...  1.74 us

commit v1 on v0

--- a/solution.py
+++ b/solution.py
@@ -13,7 +13,6 @@
 ALIGN = 16
 TILE = 256
 ROWS = 512
-LANES = 128
 
 
 def silu(u):
@@ -93,7 +92,7 @@
                 dst[half, row, PAD : PAD + wide, :] = keep * here + amount * around
             return carry
 
-        lax.fori_loop(first, last, row_step, 0)
+        lax.fori_loop(first, last, row_step, 0, unroll=2)
 
     sweep(a_buf, b_buf, 1, low + HALO - 1)
     sweep(b_buf, a_buf, 2, low + HALO - 2)
@@ -206,8 +205,8 @@
 
 def exchange(
     n_lon, state, listed, counts,
-    north, south, side, corner_n, corner_s, mask, other, above, below, above_x, below_x,
-    edges, lines, edge_sem, send_sem, recv_sem,
+    north, south, side, corner_n, corner_s, tiles,
+    mine, strip, above, below, other, above_x, below_x, edges, lines, edge_sem, send_sem, recv_sem,
 ):
     lon, lat, _ = state.shape
     place, me = lax.axis_index("lon"), lax.axis_index("lat")
@@ -256,73 +255,83 @@
     numbers = listed[...]
     length = numbers.shape[1]
     active = lax.broadcasted_iota(jnp.int32, (1, length), 1) < counts[place]
-    rows = jnp.where(active, lax.shift_right_logical(numbers, jnp.int32(lat.bit_length() - 1)), -1)
+    numbers = jnp.where(active, numbers, -1)
+    rows = lax.shift_right_arithmetic(numbers, jnp.int32(lat.bit_length() - 1))
     spots = numbers & (lat - 1)
-    row_hot = jnp.where(lax.broadcasted_iota(jnp.int32, (lon, length), 0) == rows, 1.0, 0.0)
-    spot_hot = jnp.where(lax.broadcasted_iota(jnp.int32, (LANES, length), 0) == spots, 1.0, 0.0)
-    mask[...] = lax.dot_general(
-        row_hot.astype(jnp.bfloat16), spot_hot.astype(jnp.bfloat16), (((1,), (1,)), ((), ())),
-        preferred_element_type=jnp.float32,
-    )
-    first, last = mask.at[pl.ds(0, BLOCK)], mask.at[pl.ds(lon - BLOCK, BLOCK)]
-    send(mask, other, others[2])
-    send(first, below, others[0])
-    send(last, above, others[1])
-    send(first, below_x, others[3])
-    send(last, above_x, others[4])
+
+    def hot(number, size):
+        same = lax.broadcasted_iota(jnp.int32, (size, length), 0) == number
+        return jnp.where(same, 1.0, 0.0).astype(jnp.bfloat16)
+
+    def marks(tile, position, size):
+        return lax.dot_general(
+            hot(tile, size), hot(position, TILE), (((1,), (1,)), ((), ())),
+            preferred_element_type=jnp.float32,
+        )
+
+    n_main = lon * lat // TILE
+    mine[...] = marks(
+        lax.shift_right_arithmetic(numbers, jnp.int32(TILE.bit_length() - 1)), numbers & (TILE - 1), n_main
+    )
+    height = TILE // BLOCK
+    reached = jnp.where(me == 0, lat - 2, 0)
+    close = (spots >= reached) & (spots < reached + 2)
+    strip_tile = jnp.where(
+        close, lax.shift_right_arithmetic(rows, jnp.int32(height.bit_length() - 1)), -1
+    )
+    strip[...] = marks(strip_tile, (rows & (height - 1)) * BLOCK + (spots & (BLOCK - 1)), BLOCK)
+    send(mine.at[pl.ds(0, BLOCK)], below, others[0])
+    send(mine.at[pl.ds(n_main - BLOCK, BLOCK)], above, others[1])
+    send(strip, below_x, others[3])
+    send(strip, above_x, others[4])
+    send(strip, other, others[2])
     for copy in sent:
         copy.wait()
 
-
-def take_near(rows, lat, first_lat):
-    reach = jnp.arange(BLOCK)
-    near = jnp.where(first_lat, rows[:, :BLOCK], rows[:, lat - BLOCK : lat])
-    return jnp.where(jnp.where(first_lat, reach < 2, reach >= BLOCK - 2)[None], near, 0.0)
+    n_strip = lon // height
+    lane = lax.broadcasted_iota(jnp.int32, (BLOCK, TILE), 1)
+    from_n = pltpu.roll(above_x[...], BLOCK, 1)[n_strip - 1 : n_strip]
+    from_s = pltpu.roll(below_x[...], BLOCK, 1)[0:1]
+    lane = lane[0:1]
+    tiles[0:1, :] = jnp.where(lane < BLOCK, from_n, jnp.where(lane < 2 * BLOCK, from_s, 0.0))
+    tiles[1 : 1 + n_strip, :] = other[0:n_strip, :]
+    near = 2 * lat
+    tiles[1 + n_strip : 2 + n_strip, 0:near] = above[BLOCK - 1 : BLOCK, TILE - near :]
+    tiles[1 + n_strip : 2 + n_strip, near:] = below[0:1, 0:near]
+    tiles[2 + n_strip :, :] = mine[...]
 
 
 def local(n_lon, state_in, diffusion, conv_index, conv_count, w_first, w_hidden, w_last):
     lon, lat, feat = state_in.shape
-    lat_place = lax.axis_index("lat")
-    first_lat = lat_place == 0
 
     listed = conv_index.reshape(1, -1)
-    anywhere = pl.BlockSpec(memory_space=pl.ANY)
+    anywhere = pl.BlockSpec(memory_space=pltpu.HBM)
     vmem = pl.BlockSpec(memory_space=pltpu.VMEM)
     smem = pl.BlockSpec(memory_space=pltpu.SMEM)
     shape = jax.ShapeDtypeStruct
     lines = shape((HALO, lat, feat), jnp.bfloat16)
     block = shape((HALO, BLOCK, feat), jnp.float32)
-    few = shape((BLOCK, LANES), jnp.float32)
-    full = shape((lon, LANES), jnp.float32)
-    north, south, side, corner_n, corner_s, mask, other, above, below, above_x, below_x = pl.pallas_call(
+    n_tiles = 2 + lon * BLOCK // TILE + lon * lat // TILE
+    few = pltpu.VMEM((BLOCK, TILE), jnp.float32)
+    north, south, side, corner_n, corner_s, tiles = pl.pallas_call(
         functools.partial(exchange, n_lon),
         out_shape=(lines, lines, shape((lon, BLOCK, feat), jnp.float32), block, block)
-        + (full, full, few, few, few, few),
+        + (shape((n_tiles, TILE), jnp.float32),),
         in_specs=[anywhere, vmem, smem],
-        out_specs=(anywhere,) * 5 + (vmem,) * 6,
+        out_specs=(anywhere,) * 5 + (vmem,),
         scratch_shapes=[
+            pltpu.VMEM((lon * lat // TILE, TILE), jnp.float32),
+            few, few, few, few, few, few,
             pltpu.VMEM((2, HALO, lat, feat), jnp.float32),
             pltpu.VMEM((2, HALO, lat, feat), jnp.bfloat16),
             pltpu.SemaphoreType.DMA((2,)),
             pltpu.SemaphoreType.DMA((10,)),
             pltpu.SemaphoreType.DMA((10,)),
         ],
-        compiler_params=pltpu.CompilerParams(collective_id=0, has_side_effects=True),
+        compiler_params=pltpu.CompilerParams(
+            collective_id=0, has_side_effects=True, vmem_limit_bytes=60 * 1024 * 1024
+        ),
     )(state_in, listed, conv_count[0, :, 0])
-    mask = mask[:, :lat]
-    other = other[:, :lat]
-    above = jnp.concatenate([above[BLOCK - 2 :, :lat], take_near(above_x[BLOCK - 2 :], lat, first_lat)], axis=1)
-    below = jnp.concatenate([below[:2, :lat], take_near(below_x[:2], lat, first_lat)], axis=1)
-    near = take_near(other, lat, first_lat)
-    corner = jnp.concatenate([above[1, lat:], below[0, lat:]])
-    tiles = jnp.concatenate(
-        [
-            jnp.pad(corner, (0, TILE - corner.shape[0]))[None],
-            near.reshape(-1, TILE),
-            jnp.concatenate([above[:, :lat], below[:, :lat]]).reshape(-1, TILE),
-            mask.reshape(-1, TILE),
-        ]
-    )
     spots = jnp.arange(TILE)
     ranks = jnp.dot(
         tiles.astype(jnp.bfloat16),
@@ -332,7 +341,6 @@
     keys = jnp.where(tiles > 0.5, ranks, -1.0)
     counts = tiles.sum(axis=1).astype(jnp.int32)
     counts = (counts + ALIGN - 1) // ALIGN * ALIGN
-    n_tiles = tiles.shape[0]
     order = jnp.arange(n_tiles + 1)
     offs = jnp.where(order[:n_tiles][None] < order[:, None], counts[None], 0).sum(axis=1)
 

time: 61.5 us -> 56.6 us (0.920)
  the two profiles are of different devices: /device:TPU:5 before, /device:TPU:21 now
where the time goes in v1:
time: 56.6 us; the launch traced here: 56.1 us
  Pallas kernels  49.7 us (88%)
  local copies, waits for them, and re-layouts  4.37 us (8%)
  matrix products  0.97 us (2%)
  other arithmetic  0.96 us (2%)
    pallas_call x1, Pallas kernels, local(): pl.pallas_call(kernel, out_shape=jax.ShapeDtypeStruct(state_in.shape, jnp...  36.1 us
    pallas_call x1, Pallas kernels, local(): pl.pallas_call(functools.partial(exchange, n_lon), out_shape=(lines, line...  13.6 us
    unnamed x16, local copies, waits for them, and re-layouts  4.37 us

profile of v1, /device:TPU:21, one launch (start us, length us, event | category | flops | bytes accessed | tf_op | source)
XLA Modules:
  0.0 56.1 jit_solution(9994745824597847590)
XLA Ops:
  0.0 0.0 copy-start.1
  0.0 0.0 copy-start
  0.0 0.0 copy-start.7
  0.0 13.6 %shard_map.73 = (bf16[4,64,256]{2,1,0:T(8,128)(2,1)}, bf16[4,64,256]{2,1,0:T(8,128)(2,1)}, f32[64,8,256]{2,1,0:T(8,128)}, f32[4,8,256]{2,1,0:T(8,128)}, f32[4,8,256]{2,1,0:T(8,128)}, /*index=5*/f32[20,256]{1,0:T(8,128)}) custom-call(f32[64,64,256]{2,1,0:T(8,128)} %state.3, s32[1,3072]{1,0:T(1,128)} %bitcast.5, s32[8]{0:T(128)} %bitcast.6), custom_call_target="tpu_custom_call" | custom-call | tf_op jit(solution)/shard_map/pallas_call | solution.py:316
  13.7 0.9 %reduce_sum.18 = f32[20]{0:T(128)S(1)} reduce(f32[20,256]{1,0:T(8,128)} %get-tuple-element.16, f32[]{:T(128)} %constant.21.clone.1), dimensions={1}, to_apply=%region_0.1 | reduce | flops 5100 | bytes 20564 | tf_op jit(solution)/shard_map/reduce_sum | solution.py:342
  14.5 1.0 %convolution_select_fusion.keys = f32[20,256]{1,0:T(8,128)S(1)} fusion(f32[20,256]{1,0:T(8,128)} %get-tuple-element.16), kind=kOutput, calls=%fused_computation | convolution fusion | flops 2702336 | bytes 40960 | tf_op jit(solution)/shard_map/dot_general | solution.py:336
  15.5 0.1 select_reduce_fusion.offs
  15.6 0.0 copy-done.1
  15.6 0.0 copy-done
  15.6 0.0 copy-done.7
  15.6 0.0 copy-start.2
  15.6 1.0 %copy-done.2 = f32[64,8,256]{2,1,0:T(8,128)S(1)} copy-done((f32[64,8,256]{2,1,0:T(8,128)S(1)}, f32[64,8,256]{2,1,0:T(8,128)}, u32[]{:S(2)}) %copy-start.2) | copy-done | bytes 524312
  16.7 0.0 copy-start.3
  16.7 0.9 %copy-done.3 = bf16[4,64,256]{2,1,0:T(8,128)(2,1)S(1)} copy-done((bf16[4,64,256]{2,1,0:T(8,128)(2,1)S(1)}, bf16[4,64,256]{2,1,0:T(8,128)(2,1)}, u32[]{:S(2)}) %copy-start.3) | copy-done | bytes 131096
  17.6 0.0 copy-start.4
  17.6 0.9 %copy-done.4 = bf16[4,64,256]{2,1,0:T(8,128)(2,1)S(1)} copy-done((bf16[4,64,256]{2,1,0:T(8,128)(2,1)S(1)}, bf16[4,64,256]{2,1,0:T(8,128)(2,1)}, u32[]{:S(2)}) %copy-start.4) | copy-done | bytes 131096
  18.5 0.0 copy-start.5
  18.5 0.8 %copy-done.5 = f32[4,8,256]{2,1,0:T(8,128)S(1)} copy-done((f32[4,8,256]{2,1,0:T(8,128)S(1)}, f32[4,8,256]{2,1,0:T(8,128)}, u32[]{:S(2)}) %copy-start.5) | copy-done | bytes 32792
  19.2 0.0 copy-start.6
  19.2 0.8 %copy-done.6 = f32[4,8,256]{2,1,0:T(8,128)S(1)} copy-done((f32[4,8,256]{2,1,0:T(8,128)S(1)}, f32[4,8,256]{2,1,0:T(8,128)}, u32[]{:S(2)}) %copy-start.6) | copy-done | bytes 32792
  20.0 36.1 %shard_map.74 = f32[64,64,256]{2,1,0:T(8,128)} custom-call(f32[64,64,256]{2,1,0:T(8,128)} %state.3, bf16[4,64,256]{2,1,0:T(8,128)(2,1)S(1)} %copy-done.3, bf16[4,64,256]{2,1,0:T(8,128)(2,1)S(1)} %copy-done.4, f32[64,8,256]{2,1,0:T(8,128)S(1)} %copy-done.2, f32[4,8,256]{2,1,0:T(8,128)S(1)} %copy-done.5, f32[4,8,256]{2,1,0:T(8,128)S(1)} %copy-done.6, ...), custom_call_target="tpu_custom_call" | custom-call | tf_op jit(solution)/shard_map/pallas_call | solution.py:351
  (2 shorter events, 0.0 us)
Async XLA Ops:
  0.0 15.6 %copy-start.1 = (bf16[1024,256]{1,0:T(8,128)(2,1)S(1)}, bf16[1024,256]{1,0:T(8,128)(2,1)}, u32[]{:S(2)}) copy-start(bf16[1024,256]{1,0:T(8,128)(2,1)} %w_last.1) | copy-start | bytes 1572868
  0.0 15.6 %copy-start = (bf16[256,1024]{1,0:T(8,128)(2,1)S(1)}, bf16[256,1024]{1,0:T(8,128)(2,1)}, u32[]{:S(2)}) copy-start(bf16[256,1024]{1,0:T(8,128)(2,1)} %w_first.1) | copy-start | bytes 1572868
  0.0 15.6 %copy-start.7 = (f32[256]{0:T(256)S(1)}, f32[256]{0:T(256)}, u32[]{:S(2)}) copy-start(f32[256]{0:T(256)} %param.8) | copy-start | bytes 3076
  15.6 1.0 %copy-start.2 = (f32[64,8,256]{2,1,0:T(8,128)S(1)}, f32[64,8,256]{2,1,0:T(8,128)}, u32[]{:S(2)}) copy-start(f32[64,8,256]{2,1,0:T(8,128)} %get-tuple-element.13.side) | copy-start | bytes 1572868
  16.7 0.9 %copy-start.3 = (bf16[4,64,256]{2,1,0:T(8,128)(2,1)S(1)}, bf16[4,64,256]{2,1,0:T(8,128)(2,1)}, u32[]{:S(2)}) copy-start(bf16[4,64,256]{2,1,0:T(8,128)(2,1)} %get-tuple-element.11.north) | copy-start | bytes 393220
  17.6 0.9 %copy-start.4 = (bf16[4,64,256]{2,1,0:T(8,128)(2,1)S(1)}, bf16[4,64,256]{2,1,0:T(8,128)(2,1)}, u32[]{:S(2)}) copy-start(bf16[4,64,256]{2,1,0:T(8,128)(2,1)} %get-tuple-element.12.south) | copy-start | bytes 393220
  18.5 0.8 %copy-start.5 = (f32[4,8,256]{2,1,0:T(8,128)S(1)}, f32[4,8,256]{2,1,0:T(8,128)}, u32[]{:S(2)}) copy-start(f32[4,8,256]{2,1,0:T(8,128)} %get-tuple-element.14.corner_n) | copy-start | bytes 98308
  19.2 0.8 %copy-start.6 = (f32[4,8,256]{2,1,0:T(8,128)S(1)}, f32[4,8,256]{2,1,0:T(8,128)}, u32[]{:S(2)}) copy-start(f32[4,8,256]{2,1,0:T(8,128)} %get-tuple-element.15.corner_s) | copy-start | bytes 98308

commit v2 on v1

--- a/solution.py
+++ b/solution.py
@@ -13,6 +13,7 @@
 ALIGN = 16
 TILE = 256
 ROWS = 512
+LANES = 128
 
 
 def silu(u):
@@ -77,6 +78,8 @@
             a_buf[half, row : row + HALO, pl.ds(own, lat), :] = cells
 
     def sweep(src, dst, first, last):
+        unroll = next(size for size in (4, 7, 2, 1) if (last - first) % size == 0)
+
         def row_step(row, carry):
             for half in range(2):
                 amount = diffusion[0:1, half * lanes : (half + 1) * lanes]
@@ -92,7 +95,7 @@
                 dst[half, row, PAD : PAD + wide, :] = keep * here + amount * around
             return carry
 
-        lax.fori_loop(first, last, row_step, 0, unroll=2)
+        lax.fori_loop(first, last, row_step, 0, unroll=unroll)
 
     sweep(a_buf, b_buf, 1, low + HALO - 1)
     sweep(b_buf, a_buf, 2, low + HALO - 2)
@@ -124,11 +127,11 @@
         ]
         values = jnp.concatenate(halves, axis=1)
         picked = jnp.dot(select(tile, values.shape[0]), values, preferred_element_type=jnp.float32)
-        start = pl.multiple_of(offs[tile], ALIGN)
+        start = pl.multiple_of(offs[tile, 0], ALIGN)
         packed[pl.ds(start, TILE), :] = picked.astype(jnp.bfloat16)
 
     def scatter(tile, slices):
-        start = pl.multiple_of(offs[tile], ALIGN)
+        start = pl.multiple_of(offs[tile, 0], ALIGN)
         change = packed[pl.ds(start, TILE), :]
         count = sum(rows * width for _, rows, _, width in slices)
         spread = lax.dot_general(
@@ -149,7 +152,7 @@
         gather(n_side + step, [(top + per_tile * step, per_tile, own, lat)])
         return carry
 
-    lax.fori_loop(0, n_main, main_gather, 0, unroll=2)
+    lax.fori_loop(0, n_main, main_gather, 0, unroll=4)
     for copy in weights:
         copy.wait()
 
@@ -172,7 +175,7 @@
         )
         return carry
 
-    total = offs[n_side + n_main]
+    total = offs[n_side + n_main, 0]
     lax.fori_loop(0, (total + ROWS - 1) // ROWS, network, 0)
 
     for tile, slices in enumerate(pieces):
@@ -182,9 +185,9 @@
         scatter(n_side + step, [(top + per_tile * step, per_tile, own, lat)])
         return carry
 
-    lax.fori_loop(0, n_main, main_scatter, 0, unroll=2)
-
-    sweep(a_buf, b_buf, 3, low + HALO - 3)
+    lax.fori_loop(0, n_main, main_scatter, 0, unroll=4)
+
+    sweep(a_buf, b_buf, 2, low + HALO - 2)
     parts = 4
     outs = []
     for part in range(parts):
@@ -205,8 +208,8 @@
 
 def exchange(
     n_lon, state, listed, counts,
-    north, south, side, corner_n, corner_s, tiles,
-    mine, strip, above, below, other, above_x, below_x, edges, lines, edge_sem, send_sem, recv_sem,
+    north, south, side, corner_n, corner_s, keys, offs,
+    tiles, mine, strip, above, below, other, above_x, below_x, edges, lines, edge_sem, send_sem, recv_sem,
 ):
     lon, lat, _ = state.shape
     place, me = lax.axis_index("lon"), lax.axis_index("lat")
@@ -298,7 +301,31 @@
     near = 2 * lat
     tiles[1 + n_strip : 2 + n_strip, 0:near] = above[BLOCK - 1 : BLOCK, TILE - near :]
     tiles[1 + n_strip : 2 + n_strip, near:] = below[0:1, 0:near]
-    tiles[2 + n_strip :, :] = mine[...]
+    filled = 2 + n_strip + n_main
+    tiles[2 + n_strip : filled, :] = mine[...]
+    size = tiles.shape[0]
+    if filled < size:
+        tiles[filled:, :] = jnp.zeros((size - filled, TILE), jnp.float32)
+    marked = tiles[...]
+    before = jnp.where(
+        lax.broadcasted_iota(jnp.int32, (TILE, TILE), 0) < lax.broadcasted_iota(jnp.int32, (TILE, TILE), 1),
+        1.0,
+        0.0,
+    ).astype(jnp.bfloat16)
+    ranks = jnp.dot(marked.astype(jnp.bfloat16), before, preferred_element_type=jnp.float32)
+    keys[...] = jnp.where(marked > 0.5, ranks, -1.0)
+    counts = jnp.sum(marked, axis=1, keepdims=True)
+    counts = jnp.floor((counts + (ALIGN - 1)) * (1.0 / ALIGN)) * ALIGN
+    earlier = jnp.where(
+        lax.broadcasted_iota(jnp.int32, (size, size), 1) < lax.broadcasted_iota(jnp.int32, (size, size), 0),
+        1.0,
+        0.0,
+    ).astype(jnp.bfloat16)
+    offs[...] = jnp.dot(
+        earlier,
+        jnp.broadcast_to(counts, (size, offs.shape[1])).astype(jnp.bfloat16),
+        preferred_element_type=jnp.float32,
+    ).astype(jnp.int32)
 
 
 def local(n_lon, state_in, diffusion, conv_index, conv_count, w_first, w_hidden, w_last):
@@ -312,14 +339,16 @@
     lines = shape((HALO, lat, feat), jnp.bfloat16)
     block = shape((HALO, BLOCK, feat), jnp.float32)
     n_tiles = 2 + lon * BLOCK // TILE + lon * lat // TILE
+    padded = -(-(n_tiles + 1) // 8) * 8
     few = pltpu.VMEM((BLOCK, TILE), jnp.float32)
-    north, south, side, corner_n, corner_s, tiles = pl.pallas_call(
+    north, south, side, corner_n, corner_s, keys, offs = pl.pallas_call(
         functools.partial(exchange, n_lon),
         out_shape=(lines, lines, shape((lon, BLOCK, feat), jnp.float32), block, block)
-        + (shape((n_tiles, TILE), jnp.float32),),
+        + (shape((padded, TILE), jnp.float32), shape((padded, LANES), jnp.int32)),
         in_specs=[anywhere, vmem, smem],
-        out_specs=(anywhere,) * 5 + (vmem,),
+        out_specs=(anywhere,) * 5 + (vmem, vmem),
         scratch_shapes=[
+            pltpu.VMEM((padded, TILE), jnp.float32),
             pltpu.VMEM((lon * lat // TILE, TILE), jnp.float32),
             few, few, few, few, few, few,
             pltpu.VMEM((2, HALO, lat, feat), jnp.float32),
@@ -332,18 +361,6 @@
             collective_id=0, has_side_effects=True, vmem_limit_bytes=60 * 1024 * 1024
         ),
     )(state_in, listed, conv_count[0, :, 0])
-    spots = jnp.arange(TILE)
-    ranks = jnp.dot(
-        tiles.astype(jnp.bfloat16),
-        (spots[:, None] < spots[None]).astype(jnp.bfloat16),
-        preferred_element_type=jnp.float32,
-    )
-    keys = jnp.where(tiles > 0.5, ranks, -1.0)
-    counts = tiles.sum(axis=1).astype(jnp.int32)
-    counts = (counts + ALIGN - 1) // ALIGN * ALIGN
-    order = jnp.arange(n_tiles + 1)
-    offs = jnp.where(order[:n_tiles][None] < order[:, None], counts[None], 0).sum(axis=1)
-
     room = -(-(n_tiles * TILE + TILE) // ROWS) * ROWS
     wide = lat + BLOCK + 2 * PAD
     buf = pltpu.VMEM((2, lon + 2 * HALO, wide, feat // 2), jnp.float32)
@@ -367,7 +384,7 @@
             pltpu.SemaphoreType.DMA((3,)),
             pltpu.SemaphoreType.DMA((8,)),
         ],
-        compiler_params=pltpu.CompilerParams(vmem_limit_bytes=50 * 1024 * 1024),
+        compiler_params=pltpu.CompilerParams(vmem_limit_bytes=60 * 1024 * 1024),
     )(
         state_in, north, south, side, corner_n, corner_s, diffusion[None], keys, offs,
         w_first, w_hidden, w_last,

time: 56.6 us -> 50.3 us (0.89)
  the two profiles are of different devices: /device:TPU:21 before, /device:TPU:8 now
where the time goes in v2:
time: 50.3 us; the launch traced here: 49.6 us
  Pallas kernels  49.6 us (99%)
    pallas_call x1, Pallas kernels, local(): pl.pallas_call(kernel, out_shape=jax.ShapeDtypeStruct(state_in.shape, jnp...  36.1 us
    pallas_call x1, Pallas kernels, local(): pl.pallas_call(functools.partial(exchange, n_lon), out_shape=(lines, line...  13.5 us

profile of v2, /device:TPU:8, one launch (start us, length us, event | category | flops | bytes accessed | tf_op | source)
XLA Modules:
  0.0 49.6 jit_solution(2745110432989476606)
XLA Ops:
  0.0 13.5 %shard_map.73 = (bf16[4,64,256]{2,1,0:T(8,128)(2,1)}, bf16[4,64,256]{2,1,0:T(8,128)(2,1)}, f32[64,8,256]{2,1,0:T(8,128)}, f32[4,8,256]{2,1,0:T(8,128)}, f32[4,8,...) custom-call(f32[64,64,256]{2,1,0:T(8,128)} %state.3, s32[1,3072]{1,0:T(1,128)} %bitcast.3, s32[8]{0:T(128)} %bitcast.5), custom_call_target="tpu_custom_call" | custom-call | tf_op jit(solution)/shard_map/pallas_call | solution.py:344
  13.5 36.1 %shard_map.74 = f32[64,64,256]{2,1,0:T(8,128)} custom-call(f32[64,64,256]{2,1,0:T(8,128)} %state.3, bf16[4,64,256]{2,1,0:T(8,128)(2,1)} %get-tuple-element.12.north, bf16[4,64,256]{2,1,0:T(8,128)(2,1)} %get-tuple-element.13.south, f32[64,8,256]{2,1,0:T(8,128)} %get-tuple-element.14.side, f32[4,8,256]{2,1,0:T(8,128)} %get-tuple-element.15.corner_n, ...), custom_call_target="tpu_custom_call" | custom-call | tf_op jit(solution)/shard_map/pallas_call | solution.py:368
